TPU v7x, 512 devices: a whole 4x4x16 slice. The times are simulated.
512 devices in a mesh: gx: 32 (over z_lo, y), gy: 16 (over x, z_hi, core).
Axes of the slice: x: 4, y: 4, z: 16 (z_hi: 2, z_lo: 8; z = z_hi * 8 + z_lo), core: 2. Of those that a mesh axis runs over, the one named last changes fastest.
Arguments:
- image_embeds: bfloat16 [49152, 1152], P(('gx', 'gy')), may hold values from -0.75 to 0.75
- text_embeds: bfloat16 [49152, 1152], P(('gx', 'gy')), may hold values from -0.75 to 0.75
- logit_scale: float32 [1], replicated, may hold values from 4 to 8
- logit_bias: float32 [1], replicated, may hold values from -3 to -1
Outputs:
- image_grads: float32 [49152, 1152], P(('gx', 'gy'))
- text_grads: float32 [49152, 1152], P(('gx', 'gy'))
All inputs are finite; a program needn't handle non-finite values.
Results may differ from a plain program's by a relative error of at most 0.003.
Values may be sent and summed in bfloat16 or wider, within the bound.
A program may use at most 64 MiB of HBM per device.

v0:
```python
import jax
import jax.numpy as jnp
from jax import lax
from jax.sharding import PartitionSpec as P

REACH = 1


def shifted(value, axis, steps):
    count = lax.axis_size(axis)
    pairs = [(source, (source + steps) % count) for source in range(count)]
    return lax.ppermute(value, axis, pairs)


def body(image_embeds, text_embeds, logit_scale, logit_bias):
    gain = logit_scale[0]
    offset = logit_bias[0]
    row_count = text_embeds.shape[0]
    feature_count = text_embeds.shape[1]
    cycle_size = lax.axis_size("gx")
    column_size = lax.axis_size("gy")
    here_x = lax.axis_index("gx")
    here_y = lax.axis_index("gy")
    image_column = lax.all_gather(image_embeds, "gy", axis=0, tiled=True)
    column_rows = column_size * row_count
    image_ids = here_x * column_rows + lax.iota(jnp.int32, column_rows)
    local_rows = lax.iota(jnp.int32, row_count)
    moving = shifted(text_embeds, "gx", -REACH)
    carried = jnp.zeros((row_count, feature_count), jnp.float32)
    image_partial = jnp.zeros((column_rows, feature_count), jnp.float32)
    for visit in range(2 * REACH + 1):
        last_visit = visit == 2 * REACH
        if not last_visit:
            upcoming = shifted(moving, "gx", 1)
        anchor = (here_x - (visit - REACH)) % cycle_size
        text_ids = (anchor * column_size + here_y) * row_count + local_rows
        logits = lax.dot_general(
            moving, image_column, (((1,), (1,)), ((), ())), preferred_element_type=jnp.float32
        )
        labels = (text_ids[:, None] == image_ids[None, :]).astype(jnp.float32)
        weights = (jax.nn.sigmoid(gain * logits + offset) - labels).astype(jnp.bfloat16)
        text_term = jnp.dot(weights, image_column, preferred_element_type=jnp.float32)
        image_term = lax.dot_general(
            weights, moving, (((0,), (0,)), ((), ())), preferred_element_type=jnp.float32
        )
        text_term, image_term = (text_term, image_term)
        carried = carried + text_term
        image_partial = image_partial + image_term
        if not last_visit:
            carried = shifted(carried, "gx", 1)
            moving = upcoming
    text_total = shifted(carried, "gx", -REACH)
    rounded = image_partial.astype(jnp.bfloat16).reshape(column_size, row_count, feature_count)
    arrived = lax.all_to_all(rounded, "gy", split_axis=0, concat_axis=0, tiled=True)
    image_total = jnp.sum(arrived, axis=0, dtype=jnp.float32)
    return (gain * image_total, gain * text_total)


def solution(mesh):
    in_specs = (P(("gx", "gy"), None), P(("gx", "gy"), None), P(), P())
    out_specs = (P(("gx", "gy"), None), P(("gx", "gy"), None))
    return jax.shard_map(body, mesh=mesh, in_specs=in_specs, out_specs=out_specs, check_vma=False)
```

profile of v0, /device:TPU:24, one launch (start us, length us, event | category | flops | bytes accessed | tf_op | source)
XLA Modules:
  0.0 357.3 jit_solution(7315454966297397894)
XLA Ops:
  7.2 0.0 all-gather.2.cloned.1.call-start
  7.2 0.7 all-gather.2.cloned.1.call-update
  7.9 2.7 collective-permute-start
  11.9 7.4 %collective-permute-done = bf16[96,1152]{1,0:T(8,128)(2,1)S(1)} collective-permute-done((bf16[96,1152]{1,0:T(8,128)(2,1)}, bf16[96,1152]{1,0:T(8,128)(2,1)S(1)}, u32[]{:S(2)}, u32[]{:S(2)}) %collective-permute-start) | collective-permute-done | bytes 221216 | tf_op jit(solution)/shard_map/ppermute | solution.py:12
  19.3 0.0 copy-start.6
  19.3 1.9 collective-permute-start.1
  21.2 6.3 %collective-permute-done.1 = bf16[96,1152]{1,0:T(8,128)(2,1)} collective-permute-done((bf16[96,1152]{1,0:T(8,128)(2,1)S(1)}, bf16[96,1152]{1,0:T(8,128)(2,1)}, u32[]{:S(2)}, u32[]{:S(2)}) %collective-permute-start.1) | collective-permute-done | bytes 221216 | tf_op jit(solution)/shard_map/ppermute | solution.py:12
  27.6 4.3 %collective-permute-start.2 = (bf16[96,1152]{1,0:T(8,128)(2,1)}, bf16[96,1152]{1,0:T(8,128)(2,1)}, u32[]{:S(2)}, u32[]{:S(2)}) collective-permute-start(bf16[96,1152]{1,0:T(8,128)(2,1)} %collective-permute-done.1), channel_id=1, source_target_pairs={{0,16},{16,32},{32,48},{48,64},{64,80},{80,96},{96,112},{112,128},... | collective-permute-start | bytes 663560 | tf_op jit(solution)/shard_map/ppermute | solution.py:12
  31.9 99.1 %all-gather.2.cloned.1.call-done = bf16[1536,1152]{1,0:T(8,128)(2,1)} async-done(((bf16[96,1152]{1,0:T(8,128)(2,1)}), bf16[1536,1152]{1,0:T(8,128)(2,1)}) %all-gather.2.cloned.1.call-update) | async-done | bytes 3538960 | tf_op jit(solution)/shard_map/all_gather | solution.py:24
  131.0 0.0 copy-done.6
  131.0 3.2 fusion.21
  134.3 0.0 copy-start.1
  134.3 0.0 copy-start
  134.3 2.2 fusion.22
  136.5 0.0 copy-done.1
  136.5 0.0 copy-done
  136.5 2.2 fusion.20
  138.7 0.0 copy-start.4
  138.7 2.2 convolution_add_fusion.1
  140.9 0.0 copy-done.4
  140.9 0.0 collective-permute-done.2
  140.9 2.2 fusion.19
  143.1 0.0 copy-start.2
  143.1 3.9 %fusion = bf16[1536,1152]{1,0:T(8,128)(2,1)} fusion(f32[1536,1152]{1,0:T(8,128)S(1)} %convolution_add_fusion.1, bf16[96,1536]{1,0:T(8,128)(2,1)S(1)} %fusion.19, bf16[96,1152]{1,0:T(8,128)(2,1)} %collective-permute-done.2), kind=kOutput, calls=%fused_computation.2 | convolution fusion | flops 343277568 | bytes 11132928 | tf_op jit(solution)/shard_map/dot_general | solution.py:43
  147.0 0.0 copy-done.2
  147.0 4.5 %all-to-all-start = ((bf16[16,96,1152]{2,1,0:T(8,128)(2,1)}), bf16[16,96,1152]{2,1,0:T(8,128)(2,1)}, u32[]{:S(2)}, u32[]{:S(2)}) async-start(bf16[16,96,1152]{2,1,0:T(8,128)(2,1)} %bitcast.29), calls=%async_computation | async-start | bytes 7077888 | tf_op jit(solution)/shard_map/all_to_all | solution.py:54
  151.5 0.0 copy-start.5
  151.5 0.0 copy-start.3
  151.5 1.7 fusion.23
  153.3 1.9 collective-permute-start.3
  155.2 158.6 %collective-permute-done.3 = f32[96,1152]{1,0:T(8,128)S(1)} collective-permute-done((f32[96,1152]{1,0:T(8,128)S(1)}, f32[96,1152]{1,0:T(8,128)S(1)}, u32[]{:S(2)}, u32[]{:S(2)}) %collective-permute-start.3) | collective-permute-done | bytes 442400 | tf_op jit(solution)/shard_map/ppermute | solution.py:12
  313.8 0.0 copy-done.5
  313.8 0.7 convolution_add_fusion.2
  314.6 6.5 %collective-permute-start.4 = (f32[96,1152]{1,0:T(8,128)S(1)}, f32[96,1152]{1,0:T(8,128)S(1)}, u32[]{:S(2)}, u32[]{:S(2)}) collective-permute-start(f32[96,1152]{1,0:T(8,128)S(1)} %convolution_add_fusion.2), channel_id=1, source_target_pairs={{0,16},{16,32},{32,48},{48,64},{64,80},{80,96},{96,112},{112,128},... | collective-permute-start | bytes 1327112 | tf_op jit(solution)/shard_map/ppermute | solution.py:12
  321.1 0.0 copy-done.3
  321.1 0.7 fusion.24
  321.8 8.7 %collective-permute-done.4 = f32[96,1152]{1,0:T(8,128)S(1)} collective-permute-done((f32[96,1152]{1,0:T(8,128)S(1)}, f32[96,1152]{1,0:T(8,128)S(1)}, u32[]{:S(2)}, u32[]{:S(2)}) %collective-permute-start.4) | collective-permute-done | bytes 442400 | tf_op jit(solution)/shard_map/ppermute | solution.py:12
  330.5 1.9 collective-permute-start.5
  332.4 13.8 %collective-permute-done.5 = f32[96,1152]{1,0:T(8,128)S(1)} collective-permute-done((f32[96,1152]{1,0:T(8,128)S(1)}, f32[96,1152]{1,0:T(8,128)S(1)}, u32[]{:S(2)}, u32[]{:S(2)}) %collective-permute-start.5) | collective-permute-done | bytes 442400 | tf_op jit(solution)/shard_map/ppermute | solution.py:12
  346.2 0.8 broadcast_multiply_fusion
  347.0 0.0 all-to-all-done
  347.0 2.6 convert_reduce_fusion
  349.6 0.8 broadcast_multiply_fusion.1
  (5 shorter events, 0.1 us)
Async XLA Ops:
  7.2 123.8 %all-gather.2.cloned.1.call-start = ((), (), s32[]{:S(2)}) async-start(), calls=%async_computation.1 | async-start | bytes 3760128 | tf_op jit(solution)/shard_map/all_gather | solution.py:24
  7.9 11.4 %collective-permute-start = (bf16[96,1152]{1,0:T(8,128)(2,1)}, bf16[96,1152]{1,0:T(8,128)(2,1)S(1)}, u32[]{:S(2)}, u32[]{:S(2)}) collective-permute-start(bf16[96,1152]{1,0:T(8,128)(2,1)} %param.5), channel_id=1, source_target_pairs={{0,496},{16,0},{32,16},{48,32},{64,48},{80,64},{96,80},{112,96},{1... | collective-permute-start | bytes 663560 | tf_op jit(solution)/shard_map/ppermute | solution.py:12
  19.3 111.7 %copy-start.6 = (bf16[96,1152]{1,0:T(8,128)(2,1)}, bf16[96,1152]{1,0:T(8,128)(2,1)S(1)}, u32[]{:S(2)}) copy-start(bf16[96,1152]{1,0:T(8,128)(2,1)S(1)} %collective-permute-done) | copy-start | bytes 663556
  19.3 8.3 %collective-permute-start.1 = (bf16[96,1152]{1,0:T(8,128)(2,1)S(1)}, bf16[96,1152]{1,0:T(8,128)(2,1)}, u32[]{:S(2)}, u32[]{:S(2)}) collective-permute-start(bf16[96,1152]{1,0:T(8,128)(2,1)S(1)} %collective-permute-done), channel_id=1, source_target_pairs={{0,16},{16,32},{32,48},{48,64},{64,80},{80,96},{96,112},{112,128},... | collective-permute-start | bytes 663560 | tf_op jit(solution)/shard_map/ppermute | solution.py:12
  27.6 113.3 %collective-permute-start.2 = (bf16[96,1152]{1,0:T(8,128)(2,1)}, bf16[96,1152]{1,0:T(8,128)(2,1)}, u32[]{:S(2)}, u32[]{:S(2)}) collective-permute-start(bf16[96,1152]{1,0:T(8,128)(2,1)} %collective-permute-done.1), channel_id=1, source_target_pairs={{0,16},{16,32},{32,48},{48,64},{64,80},{80,96},{96,112},{112,128},... | collective-permute-start | bytes 663560 | tf_op jit(solution)/shard_map/ppermute | solution.py:12
  134.3 2.2 copy-start.1
  134.3 2.2 copy-start
  138.7 2.2 copy-start.4
  143.1 3.9 %copy-start.2 = (bf16[96,1536]{1,0:T(8,128)(2,1)}, bf16[96,1536]{1,0:T(8,128)(2,1)S(1)}, u32[]{:S(2)}) copy-start(bf16[96,1536]{1,0:T(8,128)(2,1)S(1)} %fusion.19) | copy-start | bytes 884740
  147.0 200.0 %all-to-all-start = ((bf16[16,96,1152]{2,1,0:T(8,128)(2,1)}), bf16[16,96,1152]{2,1,0:T(8,128)(2,1)}, u32[]{:S(2)}, u32[]{:S(2)}) async-start(bf16[16,96,1152]{2,1,0:T(8,128)(2,1)} %bitcast.29), calls=%async_computation | async-start | bytes 7077888 | tf_op jit(solution)/shard_map/all_to_all | solution.py:54
  151.5 162.3 %copy-start.5 = (bf16[96,1536]{1,0:T(8,128)(2,1)S(1)}, bf16[96,1536]{1,0:T(8,128)(2,1)}, u32[]{:S(2)}) copy-start(bf16[96,1536]{1,0:T(8,128)(2,1)} %copy-done.4) | copy-start | bytes 884740
  151.5 169.5 %copy-start.3 = (bf16[96,1536]{1,0:T(8,128)(2,1)S(1)}, bf16[96,1536]{1,0:T(8,128)(2,1)}, u32[]{:S(2)}) copy-start(bf16[96,1536]{1,0:T(8,128)(2,1)} %copy-done.2) | copy-start | bytes 884740
  153.3 160.6 %collective-permute-start.3 = (f32[96,1152]{1,0:T(8,128)S(1)}, f32[96,1152]{1,0:T(8,128)S(1)}, u32[]{:S(2)}, u32[]{:S(2)}) collective-permute-start(f32[96,1152]{1,0:T(8,128)S(1)} %fusion.23), channel_id=1, source_target_pairs={{0,16},{16,32},{32,48},{48,64},{64,80},{80,96},{96,112},{112,128},... | collective-permute-start | bytes 1327112 | tf_op jit(solution)/shard_map/ppermute | solution.py:12
  314.6 15.9 %collective-permute-start.4 = (f32[96,1152]{1,0:T(8,128)S(1)}, f32[96,1152]{1,0:T(8,128)S(1)}, u32[]{:S(2)}, u32[]{:S(2)}) collective-permute-start(f32[96,1152]{1,0:T(8,128)S(1)} %convolution_add_fusion.2), channel_id=1, source_target_pairs={{0,16},{16,32},{32,48},{48,64},{64,80},{80,96},{96,112},{112,128},... | collective-permute-start | bytes 1327112 | tf_op jit(solution)/shard_map/ppermute | solution.py:12
  330.5 15.8 %collective-permute-start.5 = (f32[96,1152]{1,0:T(8,128)S(1)}, f32[96,1152]{1,0:T(8,128)S(1)}, u32[]{:S(2)}, u32[]{:S(2)}) collective-permute-start(f32[96,1152]{1,0:T(8,128)S(1)} %add.120), channel_id=1, source_target_pairs={{0,496},{16,0},{32,16},{48,32},{64,48},{80,64},{96,80},{112,96},{1... | collective-permute-start | bytes 1327112 | tf_op jit(solution)/shard_map/ppermute | solution.py:12
Sparse Core Ops, SparseCore 0:
  11.3 119.6 all-gather.1
where the time goes:
time: 363 us; the launch traced here: 357 us
  waiting for transfers between devices  295 us (81%)
  starting transfers between devices  23.7 us (7%)
  matrix products  19 us (5%)
  between operations  15.6 us (4%)
  other arithmetic  4.24 us (1%)
    ppermute x6, waiting for transfers between devices, shifted(): return lax.ppermute(value, axis, pairs)  195 us
    all_gather x1, waiting for transfers between devices, body(): image_column = lax.all_gather(image_embeds, 'gy', axis=0, tiled=True)  99.1 us
    ppermute x6, starting transfers between devices, shifted(): return lax.ppermute(value, axis, pairs)  19.2 us
    dot_general x3, matrix products, body(): lax.dot_general(weights, moving, (((0,), (0,)), ((), ())), preferred_elem...  8.27 us
    dot_general x3, matrix products, body(): lax.dot_general(moving, image_column, (((1,), (1,)), ((), ())), preferred...  7.61 us
  transfers between devices with their start and end apart: 8, of which 6 were waited for; matrix products, arithmetic and copies ran while one was open for 4% of the time, Pallas kernels for 0%

commit v1 on v0

v1 whole, which is shorter than its diff:
```python
import jax
import jax.numpy as jnp
from jax import lax
from jax.experimental import pallas as pl
from jax.experimental.pallas import tpu as pltpu
from jax.sharding import PartitionSpec as P

MESH = pl.DeviceIdType.MESH
CHUNKS = (32, 32, 32)
CHIPS_X = 4
NT = (((1,), (1,)), ((), ()))
TN = (((0,), (0,)), ((), ()))


def kernel(
    gain_ref, bias_ref, image_ref, text_ref,
    image_out, text_out,
    texts, near, far, text_sum, text_in, text_send, text_back,
    near_own, near_send, near_in, far_own, far_send, far_in, back_send, back_in,
    send_sems, recv_sems, local_sems,
):
    rows, width = image_ref.shape
    group_count = lax.axis_size("gx")
    plane_count = 2 * group_count
    here_x = lax.axis_index("gx")
    here_y = lax.axis_index("gy")
    core = here_y % 2
    chip = here_y // 4
    plane = here_x + group_count * ((here_y // 2) % 2)

    def device(plane_step, chip_step, other_core=False):
        to_plane = (plane + plane_step + plane_count) % plane_count
        to_chip = (chip + chip_step) % CHIPS_X
        to_core = 1 - core if other_core else core
        return (to_plane % group_count, to_chip * 4 + (to_plane // group_count) * 2 + to_core)

    mate = device(0, 0, True)
    across = device(group_count, 0)
    above = device(1, 0)
    below = device(-1, 0)
    side = {step: device(0, step) for step in (1, 3, 2)}

    barrier = pltpu.get_barrier_semaphore()
    partners = [across, above, below, side[1], side[2], side[3], mate]
    for partner in partners:
        pl.semaphore_signal(barrier, inc=1, device_id=partner, device_id_type=MESH)

    used = [0]
    started = []

    def send(source, target, to):
        slot = used[0]
        used[0] += 1
        copy = pltpu.make_async_remote_copy(
            src_ref=source, dst_ref=target, send_sem=send_sems.at[slot], recv_sem=recv_sems.at[slot],
            device_id=to, device_id_type=MESH,
        )
        copy.start()
        started.append(copy)
        return copy

    def block(ref, at, count=rows):
        return ref.at[pl.ds(at, count)]

    starts = [sum(CHUNKS[:k]) for k in range(len(CHUNKS))]
    own_text = pltpu.make_async_copy(text_ref, block(texts, 0), local_sems.at[0])
    own_image = pltpu.make_async_copy(image_ref, block(near, 0), local_sems.at[1])
    own_text.start()
    own_image.start()
    pl.semaphore_wait(barrier, len(partners))

    outward = [
        send(block(image_ref, at, count), block(far, 4 * at, count), across)
        for at, count in zip(starts, CHUNKS)
    ]
    up = send(text_ref, block(texts, 2 * rows), above)
    down = send(text_ref, block(texts, rows), below)
    to_mate = send(text_ref, block(texts, 3 * rows), mate)
    spread = [send(image_ref, block(near, (4 - step) * rows), side[step]) for step in side]

    up.wait_recv()
    passed_up = send(block(texts, 2 * rows), block(texts, 5 * rows), mate)
    down.wait_recv()
    passed_down = send(block(texts, rows), block(texts, 4 * rows), mate)

    gathers = {}

    def gather(k):
        at, count = starts[k], CHUNKS[k]
        outward[k].wait_recv()
        gathers[k] = [
            send(block(far, 4 * at, count), block(far, 4 * at + (4 - step) * count, count), side[step])
            for step in side
        ]

    gain = gain_ref[0]
    bias = bias_ref[0]

    def weights_of(images, own):
        logits = lax.dot_general(images, texts[...], NT, preferred_element_type=jnp.float32)
        weights = jax.nn.sigmoid(gain * logits + bias)
        if own:
            row = lax.broadcasted_iota(jnp.int32, logits.shape, 0)
            column = lax.broadcasted_iota(jnp.int32, logits.shape, 1)
            weights = weights - jnp.logical_and(row == column, row < rows).astype(jnp.float32)
        return weights.astype(jnp.bfloat16)

    gather(0)
    own_text.wait()
    own_image.wait()
    for copy in spread + [to_mate, passed_up, passed_down]:
        copy.wait_recv()

    images = near[...]
    weights = weights_of(images, True)
    text_sum[...] = lax.dot_general(weights, images, TN, preferred_element_type=jnp.float32)
    partial = jnp.dot(weights, texts[...], preferred_element_type=jnp.float32)
    near_own[...] = partial[:rows]
    near_send[...] = partial[rows:].astype(jnp.bfloat16)

    scatters = {}
    returns = {}

    def work(k):
        at, count = starts[k], CHUNKS[k]
        for copy in gathers[k]:
            copy.wait_recv()
        images = far[pl.ds(4 * at, 4 * count), :]
        weights = weights_of(images, False)
        partial = jnp.dot(weights, texts[...], preferred_element_type=jnp.float32)
        far_own[pl.ds(at, count), :] = partial[:count]
        far_send[pl.ds(3 * at, 3 * count), :] = partial[count:].astype(jnp.bfloat16)
        scatters[k] = [
            send(
                block(far_send, 3 * at + (step - 1) * count, count),
                block(far_in, 3 * at + (3 - step) * count, count),
                side[step],
            )
            for step in side
        ]
        text_sum[...] += lax.dot_general(weights, images, TN, preferred_element_type=jnp.float32)

    def give_back(k):
        at, count = starts[k], CHUNKS[k]
        for copy in scatters[k]:
            copy.wait_recv()
        total = far_own[pl.ds(at, count), :]
        for step in range(3):
            total = total + far_in[pl.ds(3 * at + step * count, count), :].astype(jnp.float32)
        back_send[pl.ds(at, count), :] = total.astype(jnp.bfloat16)
        returns[k] = send(block(back_send, at, count), block(back_in, at, count), across)

    last = len(CHUNKS) - 1
    if last >= 1:
        gather(1)
    for k in range(last + 1):
        work(k)
        if k + 2 <= last:
            gather(k + 2)
        if k >= 1:
            give_back(k - 1)
    to_core = send(block(text_sum, 3 * rows, 3 * rows), text_in, mate)
    near_scatter = [
        send(block(near_send, (step - 1) * rows), block(near_in, (3 - step) * rows), side[step]) for step in side
    ]
    give_back(last)

    to_core.wait_recv()
    for step in (0, 1):
        part = pl.ds((step + 1) * rows, rows)
        text_send[pl.ds(step * rows, rows), :] = (text_sum[part, :] + text_in[part, :]).astype(jnp.bfloat16)
    text_up = send(block(text_send, 0), block(text_back, 0), above)
    text_down = send(block(text_send, rows), block(text_back, rows), below)

    for copy in near_scatter:
        copy.wait_recv()
    total = near_own[...]
    for step in range(3):
        total = total + near_in[pl.ds(step * rows, rows), :].astype(jnp.float32)
    near_own[...] = total

    text_up.wait_recv()
    text_down.wait_recv()
    text_out[...] = (
        text_sum[pl.ds(0, rows), :]
        + text_in[pl.ds(0, rows), :]
        + text_back[pl.ds(0, rows), :].astype(jnp.float32)
        + text_back[pl.ds(rows, rows), :].astype(jnp.float32)
    )
    for k in range(last + 1):
        part = pl.ds(starts[k], CHUNKS[k])
        returns[k].wait_recv()
        image_out[part, :] = near_own[part, :] + back_in[part, :].astype(jnp.float32)
    for copy in started:
        copy.wait_send()


def body(image_embeds, text_embeds, logit_scale, logit_bias):
    rows, width = image_embeds.shape
    copies = 1 * len(CHUNKS) + 3 + 3 + 2 + 3 * len(CHUNKS) * 2 + len(CHUNKS) + 1 + 3 + 2
    half = lambda count: pltpu.VMEM((count * rows, width), jnp.bfloat16)
    full = lambda count: pltpu.VMEM((count * rows, width), jnp.float32)
    smem = pl.BlockSpec(memory_space=pltpu.SMEM)
    anywhere = pl.BlockSpec(memory_space=pl.ANY)
    vmem = pl.BlockSpec(memory_space=pltpu.VMEM)
    image_total, text_total = pl.pallas_call(
        kernel,
        out_shape=[jax.ShapeDtypeStruct((rows, width), jnp.float32)] * 2,
        in_specs=[smem, smem, anywhere, anywhere],
        out_specs=[vmem, vmem],
        scratch_shapes=[
            half(6), half(4), half(4), full(6), full(3), half(2), half(2),
            full(1), half(3), half(3), full(1), half(3), half(3), half(1), half(1),
            pltpu.SemaphoreType.DMA((copies,)),
            pltpu.SemaphoreType.DMA((copies,)),
            pltpu.SemaphoreType.DMA((2,)),
        ],
        compiler_params=pltpu.CompilerParams(
            collective_id=0, has_side_effects=True, vmem_limit_bytes=48 * 2**20
        ),
        cost_estimate=pl.CostEstimate(
            flops=18 * 96 * 1536 * 1152, bytes_accessed=8 * 96 * 1152 * 2, transcendentals=3 * 96 * 1536
        ),
    )(logit_scale, logit_bias, image_embeds, text_embeds)
    gain = logit_scale[0]
    return (gain * image_total, gain * text_total)


def solution(mesh):
    in_specs = (P(("gx", "gy"), None), P(("gx", "gy"), None), P(), P())
    out_specs = (P(("gx", "gy"), None), P(("gx", "gy"), None))
    return jax.shard_map(body, mesh=mesh, in_specs=in_specs, out_specs=out_specs, check_vma=False)
```

time: 363 us -> 88.4 us (0.24); the launches traced: 357 us -> 87.7 us
  waiting for transfers between devices: 295 us -> 0 us
  Pallas kernels: 0 us -> 82.9 us
  starting transfers between devices: 23.7 us -> 0 us
  matrix products: 19 us -> 0 us
  between operations: 15.6 us -> 1.94 us
    ppermute x6 -> x0, waiting for transfers between devices: 195 us -> none  [shifted(): return lax.ppermute(value, axis, pairs)]
    all_gather x1 -> x0, waiting for transfers between devices: 99.1 us -> none  [body(): image_column = lax.all_gather(image_embeds, 'gy', axis=0, tiled=True)]
    pallas_call x0 -> x1, Pallas kernels: none -> 82.9 us  [body(): pl.pallas_call(kernel, out_shape=[jax.ShapeDtypeStruct((rows, width), jnp...]
    ppermute x6 -> x0, starting transfers between devices: 19.2 us -> none  [shifted(): return lax.ppermute(value, axis, pairs)]
    dot_general x9 -> x0, matrix products: 19 us -> none  [the longest x3 8.27 us: body(): lax.dot_general(weights, moving, (((0,), (0,)), ((), ())), preferred_elem...]
    all_to_all x1 -> x0, starting transfers between devices: 4.49 us -> none  [body(): lax.all_to_all(rounded, 'gy', split_axis=0, concat_axis=0, tiled=True)]
  transfers between devices with their start and end apart: 8 -> 0, of which waited for: 6 -> 0; matrix products, arithmetic and copies ran while one was open for 4% -> 0% of each run, Pallas kernels for 0% -> 0%
where the time goes in v1:
time: 88.4 us; the launch traced here: 87.7 us
  Pallas kernels  82.9 us (94%)
  between operations  1.94 us (2%)
  local copies, waits for them, and re-layouts  1.86 us (2%)
  other arithmetic  0.97 us (1%)
    pallas_call x1, Pallas kernels, body(): pl.pallas_call(kernel, out_shape=[jax.ShapeDtypeStruct((rows, width), jnp...  82.9 us
    unnamed x4, local copies, waits for them, and re-layouts  1.86 us

profile of v1, /device:TPU:24, one launch (start us, length us, event | category | flops | bytes accessed | tf_op | source)
XLA Modules:
  0.0 87.7 jit_solution(9439464537292210776)
XLA Ops:
  1.9 0.0 copy-start
  1.9 0.9 %copy-done = bf16[96,1152]{1,0:T(8,128)(2,1)S(1)} copy-done((bf16[96,1152]{1,0:T(8,128)(2,1)S(1)}, bf16[96,1152]{1,0:T(8,128)(2,1)}, u32[]{:S(2)}) %copy-start) | copy-done | bytes 221208
  2.9 0.0 copy-start.1
  2.9 0.9 %copy-done.1 = bf16[96,1152]{1,0:T(8,128)(2,1)S(1)} copy-done((bf16[96,1152]{1,0:T(8,128)(2,1)S(1)}, bf16[96,1152]{1,0:T(8,128)(2,1)}, u32[]{:S(2)}) %copy-start.1) | copy-done | bytes 221208
  3.8 82.9 %shard_map.59 = (f32[96,1152]{1,0:T(8,128)S(1)}, f32[96,1152]{1,0:T(8,128)S(1)}) custom-call(f32[1]{0:T(128)} %copy.6.gain_ref, f32[1]{0:T(128)S(6)} %copy.7.bias_ref, bf16[96,1152]{1,0:T(8,128)(2,1)S(1)} %copy-done, bf16[96,1152]{1,0:T(8,128)(2,1)S(1)} %copy-done.1), custom_call_target="tpu_custom_call" | custom-call | flops 3057647616 | bytes 1769472 | tf_op jit(solution)/shard_map/pallas_call | solution.py:206
  86.7 1.0 %broadcast_multiply_fusion = (f32[96,1152]{1,0:T(8,128)}, f32[96,1152]{1,0:T(8,128)}) fusion(f32[96,1152]{1,0:T(8,128)S(1)} %get-tuple-element.5, f32[]{:T(128)} %bitcast.1, f32[96,1152]{1,0:T(8,128)S(1)} %get-tuple-element.4), kind=kLoop, calls=%fused_computation | loop fusion | flops 221184 | bytes 1769476 | tf_op jit(solution)/shard_map/mul | solution.py:226
Async XLA Ops:
  1.9 0.9 %copy-start = (bf16[96,1152]{1,0:T(8,128)(2,1)S(1)}, bf16[96,1152]{1,0:T(8,128)(2,1)}, u32[]{:S(2)}) copy-start(bf16[96,1152]{1,0:T(8,128)(2,1)} %image_ref.1) | copy-start | bytes 663556
  2.9 0.9 %copy-start.1 = (bf16[96,1152]{1,0:T(8,128)(2,1)S(1)}, bf16[96,1152]{1,0:T(8,128)(2,1)}, u32[]{:S(2)}) copy-start(bf16[96,1152]{1,0:T(8,128)(2,1)} %text_ref.1) | copy-start | bytes 663556

commit v2 on v1

--- a/solution.py
+++ b/solution.py
@@ -6,7 +6,8 @@
 from jax.sharding import PartitionSpec as P
 
 MESH = pl.DeviceIdType.MESH
-CHUNKS = (32, 32, 32)
+CHUNKS = (16, 16, 16, 16, 16, 16)
+RELAYED = 48
 CHIPS_X = 4
 NT = (((1,), (1,)), ((), ()))
 TN = (((0,), (0,)), ((), ()))
@@ -16,7 +17,7 @@
     gain_ref, bias_ref, image_ref, text_ref,
     image_out, text_out,
     texts, near, far, text_sum, text_in, text_send, text_back,
-    near_own, near_send, near_in, far_own, far_send, far_in, back_send, back_in,
+    relay, near_own, near_send, near_in, far_own, far_send, far_in, back_send, back_in,
     send_sems, recv_sems, local_sems,
 ):
     rows, width = image_ref.shape
@@ -38,10 +39,21 @@
     across = device(group_count, 0)
     above = device(1, 0)
     below = device(-1, 0)
+    line = plane % 4
+    here_z = plane // 4
+
+    def at_plane(line_step, z_step):
+        to_line = (line + line_step + 4) % 4
+        to_z = (here_z + z_step + plane_count // 4) % (plane_count // 4)
+        to_plane = 4 * to_z + to_line
+        return (to_plane % group_count, chip * 4 + (to_plane // group_count) * 2 + core)
+
+    line_up, line_down = at_plane(1, 0), at_plane(-1, 0)
+    z_up, z_down = at_plane(0, 1), at_plane(0, -1)
     side = {step: device(0, step) for step in (1, 3, 2)}
 
     barrier = pltpu.get_barrier_semaphore()
-    partners = [across, above, below, side[1], side[2], side[3], mate]
+    partners = [across, above, below, side[1], side[2], side[3], mate, line_up, line_down, z_up, z_down]
     for partner in partners:
         pl.semaphore_signal(barrier, inc=1, device_id=partner, device_id_type=MESH)
 
@@ -62,6 +74,46 @@
     def block(ref, at, count=rows):
         return ref.at[pl.ds(at, count)]
 
+    def remote(source, target, send_at, recv_at, to):
+        return pltpu.make_async_remote_copy(
+            src_ref=source, dst_ref=target, send_sem=send_sems.at[send_at], recv_sem=recv_sems.at[recv_at],
+            device_id=to, device_id_type=MESH,
+        )
+
+    relays = []
+
+    def shift(source, target, upward):
+        to_plane, same_z, at_z = (above, line_up, z_up) if upward else (below, line_down, z_down)
+        leaves, passes = (line == 3, line == 0) if upward else (line == 0, line == 3)
+        stop = block(relay, len(relays) * RELAYED, RELAYED)
+        straight = send(block(source, 0, rows - RELAYED), block(target, 0, rows - RELAYED), to_plane)
+        first, second = used[0], used[0] + 1
+        used[0] += 2
+        part = block(source, rows - RELAYED, RELAYED)
+        rest = block(target, rows - RELAYED, RELAYED)
+        plain = remote(part, rest, first, first, to_plane)
+        detour = remote(part, stop, first, second, same_z)
+        onward = remote(stop, rest, second, first, at_z)
+        pl.when(jnp.logical_not(leaves))(plain.start)
+        pl.when(leaves)(detour.start)
+        relays.append(None)
+
+        def pass_on():
+            @pl.when(passes)
+            def _():
+                detour.wait_recv()
+                onward.start()
+
+        def arrived():
+            straight.wait_recv()
+            plain.wait_recv()
+
+        def sent():
+            plain.wait_send()
+            pl.when(passes)(onward.wait_send)
+
+        return pass_on, arrived, sent
+
     starts = [sum(CHUNKS[:k]) for k in range(len(CHUNKS))]
     own_text = pltpu.make_async_copy(text_ref, block(texts, 0), local_sems.at[0])
     own_image = pltpu.make_async_copy(image_ref, block(near, 0), local_sems.at[1])
@@ -69,19 +121,23 @@
     own_image.start()
     pl.semaphore_wait(barrier, len(partners))
 
-    outward = [
-        send(block(image_ref, at, count), block(far, 4 * at, count), across)
-        for at, count in zip(starts, CHUNKS)
-    ]
-    up = send(text_ref, block(texts, 2 * rows), above)
-    down = send(text_ref, block(texts, rows), below)
+    def go_out(k):
+        at, count = starts[k], CHUNKS[k]
+        return send(block(image_ref, at, count), block(far, 4 * at, count), across)
+
+    outward = [go_out(0)]
+    up = shift(text_ref, block(texts, 2 * rows), True)
+    down = shift(text_ref, block(texts, rows), False)
     to_mate = send(text_ref, block(texts, 3 * rows), mate)
     spread = [send(image_ref, block(near, (4 - step) * rows), side[step]) for step in side]
 
-    up.wait_recv()
+    up[0]()
+    down[0]()
+    up[1]()
     passed_up = send(block(texts, 2 * rows), block(texts, 5 * rows), mate)
-    down.wait_recv()
+    down[1]()
     passed_down = send(block(texts, rows), block(texts, 4 * rows), mate)
+    outward += [go_out(k) for k in range(1, len(CHUNKS))]
 
     gathers = {}
 
@@ -169,8 +225,8 @@
     for step in (0, 1):
         part = pl.ds((step + 1) * rows, rows)
         text_send[pl.ds(step * rows, rows), :] = (text_sum[part, :] + text_in[part, :]).astype(jnp.bfloat16)
-    text_up = send(block(text_send, 0), block(text_back, 0), above)
-    text_down = send(block(text_send, rows), block(text_back, rows), below)
+    text_up = shift(block(text_send, 0), block(text_back, 0), True)
+    text_down = shift(block(text_send, rows), block(text_back, rows), False)
 
     for copy in near_scatter:
         copy.wait_recv()
@@ -179,8 +235,10 @@
         total = total + near_in[pl.ds(step * rows, rows), :].astype(jnp.float32)
     near_own[...] = total
 
-    text_up.wait_recv()
-    text_down.wait_recv()
+    text_up[0]()
+    text_down[0]()
+    text_up[1]()
+    text_down[1]()
     text_out[...] = (
         text_sum[pl.ds(0, rows), :]
         + text_in[pl.ds(0, rows), :]
@@ -193,15 +251,17 @@
         image_out[part, :] = near_own[part, :] + back_in[part, :].astype(jnp.float32)
     for copy in started:
         copy.wait_send()
+    for move in (up, down, text_up, text_down):
+        move[2]()
 
 
 def body(image_embeds, text_embeds, logit_scale, logit_bias):
     rows, width = image_embeds.shape
-    copies = 1 * len(CHUNKS) + 3 + 3 + 2 + 3 * len(CHUNKS) * 2 + len(CHUNKS) + 1 + 3 + 2
+    copies = len(CHUNKS) + 12 + 3 + 3 + 3 * len(CHUNKS) * 2 + len(CHUNKS) + 1 + 3 + 2
     half = lambda count: pltpu.VMEM((count * rows, width), jnp.bfloat16)
     full = lambda count: pltpu.VMEM((count * rows, width), jnp.float32)
     smem = pl.BlockSpec(memory_space=pltpu.SMEM)
-    anywhere = pl.BlockSpec(memory_space=pl.ANY)
+    anywhere = pl.BlockSpec(memory_space=pltpu.HBM)
     vmem = pl.BlockSpec(memory_space=pltpu.VMEM)
     image_total, text_total = pl.pallas_call(
         kernel,
@@ -210,7 +270,7 @@
         out_specs=[vmem, vmem],
         scratch_shapes=[
             half(6), half(4), half(4), full(6), full(3), half(2), half(2),
-            full(1), half(3), half(3), full(1), half(3), half(3), half(1), half(1),
+            half(2), full(1), half(3), half(3), full(1), half(3), half(3), half(1), half(1),
             pltpu.SemaphoreType.DMA((copies,)),
             pltpu.SemaphoreType.DMA((copies,)),
             pltpu.SemaphoreType.DMA((2,)),

time: 88.4 us -> 79.5 us (0.90)
  the two profiles are of different devices: /device:TPU:24 before, /device:TPU:32 now
where the time goes in v2:
time: 79.5 us; the launch traced here: 79.3 us
  Pallas kernels  74.5 us (94%)
  between operations  1.94 us (2%)
  local copies, waits for them, and re-layouts  1.86 us (2%)
  other arithmetic  0.97 us (1%)
    pallas_call x1, Pallas kernels, body(): pl.pallas_call(kernel, out_shape=[jax.ShapeDtypeStruct((rows, width), jnp...  74.5 us
    unnamed x4, local copies, waits for them, and re-layouts  1.86 us

profile of v2, /device:TPU:32, one launch (start us, length us, event | category | flops | bytes accessed | tf_op | source)
XLA Modules:
  0.0 79.3 jit_solution(5247328532600760388)
XLA Ops:
  1.9 0.0 copy-start
  1.9 0.9 %copy-done = bf16[96,1152]{1,0:T(8,128)(2,1)S(1)} copy-done((bf16[96,1152]{1,0:T(8,128)(2,1)S(1)}, bf16[96,1152]{1,0:T(8,128)(2,1)}, u32[]{:S(2)}) %copy-start) | copy-done | bytes 221208
  2.9 0.0 copy-start.1
  2.9 0.9 %copy-done.1 = bf16[96,1152]{1,0:T(8,128)(2,1)S(1)} copy-done((bf16[96,1152]{1,0:T(8,128)(2,1)S(1)}, bf16[96,1152]{1,0:T(8,128)(2,1)}, u32[]{:S(2)}) %copy-start.1) | copy-done | bytes 221208
  3.8 74.5 %shard_map.59 = (f32[96,1152]{1,0:T(8,128)S(1)}, f32[96,1152]{1,0:T(8,128)S(1)}) custom-call(f32[1]{0:T(128)} %copy.6.gain_ref, f32[1]{0:T(128)S(6)} %copy.7.bias_ref, bf16[96,1152]{1,0:T(8,128)(2,1)S(1)} %copy-done, bf16[96,1152]{1,0:T(8,128)(2,1)S(1)} %copy-done.1), custom_call_target="tpu_custom_call" | custom-call | flops 3057647616 | bytes 1769472 | tf_op jit(solution)/shard_map/pallas_call | solution.py:266
  78.3 1.0 %broadcast_multiply_fusion = (f32[96,1152]{1,0:T(8,128)}, f32[96,1152]{1,0:T(8,128)}) fusion(f32[96,1152]{1,0:T(8,128)S(1)} %get-tuple-element.5, f32[]{:T(128)} %bitcast.1, f32[96,1152]{1,0:T(8,128)S(1)} %get-tuple-element.4), kind=kLoop, calls=%fused_computation | loop fusion | flops 221184 | bytes 1769476 | tf_op jit(solution)/shard_map/mul | solution.py:286
Async XLA Ops:
  1.9 0.9 %copy-start = (bf16[96,1152]{1,0:T(8,128)(2,1)S(1)}, bf16[96,1152]{1,0:T(8,128)(2,1)}, u32[]{:S(2)}) copy-start(bf16[96,1152]{1,0:T(8,128)(2,1)} %image_ref.1) | copy-start | bytes 663556
  2.9 0.9 %copy-start.1 = (bf16[96,1152]{1,0:T(8,128)(2,1)S(1)}, bf16[96,1152]{1,0:T(8,128)(2,1)}, u32[]{:S(2)}) copy-start(bf16[96,1152]{1,0:T(8,128)(2,1)} %text_ref.1) | copy-start | bytes 663556

commit v3 on v2

--- a/solution.py
+++ b/solution.py
@@ -8,6 +8,7 @@
 MESH = pl.DeviceIdType.MESH
 CHUNKS = (16, 16, 16, 16, 16, 16)
 RELAYED = 48
+RELAYED_LATE = 48
 CHIPS_X = 4
 NT = (((1,), (1,)), ((), ()))
 TN = (((0,), (0,)), ((), ()))
@@ -16,7 +17,7 @@
 def kernel(
     gain_ref, bias_ref, image_ref, text_ref,
     image_out, text_out,
-    texts, near, far, text_sum, text_in, text_send, text_back,
+    texts, near, far, text_sum, text_in, core_send, core_in, text_send, text_back,
     relay, near_own, near_send, near_in, far_own, far_send, far_in, back_send, back_in,
     send_sems, recv_sems, local_sems,
 ):
@@ -50,25 +51,30 @@
 
     line_up, line_down = at_plane(1, 0), at_plane(-1, 0)
     z_up, z_down = at_plane(0, 1), at_plane(0, -1)
+    skip_up, skip_down = at_plane(2, 1), at_plane(2, -1)
     side = {step: device(0, step) for step in (1, 3, 2)}
 
     barrier = pltpu.get_barrier_semaphore()
-    partners = [across, above, below, side[1], side[2], side[3], mate, line_up, line_down, z_up, z_down]
+    partners = [across, above, below, side[1], side[2], side[3], mate, line_up, line_down, z_up, z_down, skip_up, skip_down]
     for partner in partners:
         pl.semaphore_signal(barrier, inc=1, device_id=partner, device_id_type=MESH)
 
     used = [0]
     started = []
 
-    def send(source, target, to):
+    def prepare(source, target, to):
         slot = used[0]
         used[0] += 1
         copy = pltpu.make_async_remote_copy(
             src_ref=source, dst_ref=target, send_sem=send_sems.at[slot], recv_sem=recv_sems.at[slot],
             device_id=to, device_id_type=MESH,
         )
+        started.append(copy)
+        return copy
+
+    def send(source, target, to):
+        copy = prepare(source, target, to)
         copy.start()
-        started.append(copy)
         return copy
 
     def block(ref, at, count=rows):
@@ -82,21 +88,28 @@
 
     relays = []
 
-    def shift(source, target, upward):
-        to_plane, same_z, at_z = (above, line_up, z_up) if upward else (below, line_down, z_down)
-        leaves, passes = (line == 3, line == 0) if upward else (line == 0, line == 3)
-        stop = block(relay, len(relays) * RELAYED, RELAYED)
-        straight = send(block(source, 0, rows - RELAYED), block(target, 0, rows - RELAYED), to_plane)
+    def shift(source, target, upward, late):
+        count = RELAYED_LATE if late else RELAYED
+        if late:
+            to_plane, first_stop, onward_to = (above, line_down, skip_up) if upward else (below, line_up, skip_down)
+        else:
+            to_plane, first_stop, onward_to = (above, line_up, z_up) if upward else (below, line_down, z_down)
+        leaves = line == (3 if upward else 0)
+        passes = line == ((2 if upward else 1) if late else (0 if upward else 3))
+        stop = block(relay, sum(relays), count)
+        straight = None
+        if count < rows:
+            straight = send(block(source, 0, rows - count), block(target, 0, rows - count), to_plane)
         first, second = used[0], used[0] + 1
         used[0] += 2
-        part = block(source, rows - RELAYED, RELAYED)
-        rest = block(target, rows - RELAYED, RELAYED)
+        part = block(source, rows - count, count)
+        rest = block(target, rows - count, count)
         plain = remote(part, rest, first, first, to_plane)
-        detour = remote(part, stop, first, second, same_z)
-        onward = remote(stop, rest, second, first, at_z)
+        detour = remote(part, stop, first, second, first_stop)
+        onward = remote(stop, rest, second, first, onward_to)
         pl.when(jnp.logical_not(leaves))(plain.start)
         pl.when(leaves)(detour.start)
-        relays.append(None)
+        relays.append(count)
 
         def pass_on():
             @pl.when(passes)
@@ -105,7 +118,8 @@
                 onward.start()
 
         def arrived():
-            straight.wait_recv()
+            if straight is not None:
+                straight.wait_recv()
             plain.wait_recv()
 
         def sent():
@@ -123,21 +137,19 @@
 
     def go_out(k):
         at, count = starts[k], CHUNKS[k]
-        return send(block(image_ref, at, count), block(far, 4 * at, count), across)
-
-    outward = [go_out(0)]
-    up = shift(text_ref, block(texts, 2 * rows), True)
-    down = shift(text_ref, block(texts, rows), False)
+        return prepare(block(image_ref, at, count), block(far, 4 * at, count), across)
+
+    outward = [go_out(k) for k in range(len(CHUNKS))]
+
+    def further_out(k):
+        outward[k].start()
+
+    further_out(0)
+    further_out(1)
+    up = shift(text_ref, block(texts, 2 * rows), True, False)
+    down = shift(text_ref, block(texts, rows), False, False)
     to_mate = send(text_ref, block(texts, 3 * rows), mate)
     spread = [send(image_ref, block(near, (4 - step) * rows), side[step]) for step in side]
-
-    up[0]()
-    down[0]()
-    up[1]()
-    passed_up = send(block(texts, 2 * rows), block(texts, 5 * rows), mate)
-    down[1]()
-    passed_down = send(block(texts, rows), block(texts, 4 * rows), mate)
-    outward += [go_out(k) for k in range(1, len(CHUNKS))]
 
     gathers = {}
 
@@ -160,19 +172,6 @@
             column = lax.broadcasted_iota(jnp.int32, logits.shape, 1)
             weights = weights - jnp.logical_and(row == column, row < rows).astype(jnp.float32)
         return weights.astype(jnp.bfloat16)
-
-    gather(0)
-    own_text.wait()
-    own_image.wait()
-    for copy in spread + [to_mate, passed_up, passed_down]:
-        copy.wait_recv()
-
-    images = near[...]
-    weights = weights_of(images, True)
-    text_sum[...] = lax.dot_general(weights, images, TN, preferred_element_type=jnp.float32)
-    partial = jnp.dot(weights, texts[...], preferred_element_type=jnp.float32)
-    near_own[...] = partial[:rows]
-    near_send[...] = partial[rows:].astype(jnp.bfloat16)
 
     scatters = {}
     returns = {}
@@ -207,41 +206,103 @@
         returns[k] = send(block(back_send, at, count), block(back_in, at, count), across)
 
     last = len(CHUNKS) - 1
-    if last >= 1:
-        gather(1)
-    for k in range(last + 1):
-        work(k)
-        if k + 2 <= last:
-            gather(k + 2)
-        if k >= 1:
-            give_back(k - 1)
-    to_core = send(block(text_sum, 3 * rows, 3 * rows), text_in, mate)
-    near_scatter = [
-        send(block(near_send, (step - 1) * rows), block(near_in, (3 - step) * rows), side[step]) for step in side
-    ]
-    give_back(last)
-
-    to_core.wait_recv()
-    for step in (0, 1):
-        part = pl.ds((step + 1) * rows, rows)
-        text_send[pl.ds(step * rows, rows), :] = (text_sum[part, :] + text_in[part, :]).astype(jnp.bfloat16)
-    text_up = shift(block(text_send, 0), block(text_back, 0), True)
-    text_down = shift(block(text_send, rows), block(text_back, rows), False)
-
-    for copy in near_scatter:
-        copy.wait_recv()
-    total = near_own[...]
-    for step in range(3):
-        total = total + near_in[pl.ds(step * rows, rows), :].astype(jnp.float32)
-    near_own[...] = total
-
-    text_up[0]()
-    text_down[0]()
-    text_up[1]()
-    text_down[1]()
+    held = {}
+
+    def pass_on():
+        up[0]()
+        down[0]()
+
+    def text_from_below():
+        up[1]()
+        held["up"] = send(block(texts, 2 * rows), block(texts, 5 * rows), mate)
+
+    def text_from_above():
+        down[1]()
+        held["down"] = send(block(texts, rows), block(texts, 4 * rows), mate)
+
+    def work_near():
+        own_text.wait()
+        own_image.wait()
+        for copy in spread + [to_mate, held["up"], held["down"]]:
+            copy.wait_recv()
+        images = near[...]
+        weights = weights_of(images, True)
+        partial = jnp.dot(weights, texts[...], preferred_element_type=jnp.float32)
+        near_own[...] = partial[:rows]
+        near_send[...] = partial[rows:].astype(jnp.bfloat16)
+        text_sum[...] = lax.dot_general(weights, images, TN, preferred_element_type=jnp.float32)
+
+    def near_scatter():
+        held["near"] = [
+            send(block(near_send, (step - 1) * rows), block(near_in, (3 - step) * rows), side[step]) for step in side
+        ]
+
+    def text_to_core():
+        core_send[...] = text_sum[pl.ds(4 * rows, 2 * rows), :].astype(jnp.bfloat16)
+        held["core"] = send(core_send, core_in, mate)
+        held["core_own"] = send(block(text_sum, 3 * rows), text_in, mate)
+
+    moves = []
+
+    def text_moves():
+        held["core"].wait_recv()
+        for step in (0, 1):
+            part = pl.ds((step + 1) * rows, rows)
+            text_send[pl.ds(step * rows, rows), :] = (
+                text_sum[part, :] + core_in[pl.ds(step * rows, rows), :].astype(jnp.float32)
+            ).astype(jnp.bfloat16)
+            moves.append(shift(block(text_send, step * rows), block(text_back, step * rows), step == 0, True))
+
+    def text_pass_on():
+        for move in moves:
+            move[0]()
+
+    def near_sum():
+        for copy in held["near"]:
+            copy.wait_recv()
+        total = near_own[...]
+        for step in range(3):
+            total = total + near_in[pl.ds(step * rows, rows), :].astype(jnp.float32)
+        near_own[...] = total
+
+    pass_on()
+    text_from_below()
+    text_from_above()
+    further_out(2)
+    further_out(3)
+    further_out(4)
+    further_out(5)
+    gather(0)
+    gather(1)
+    work_near()
+    gather(2)
+    work(0)
+    gather(3)
+    work(1)
+    give_back(0)
+    gather(4)
+    work(2)
+    give_back(1)
+    gather(5)
+    work(3)
+    give_back(2)
+    work(4)
+    give_back(3)
+    work(5)
+    text_to_core()
+    give_back(4)
+    near_scatter()
+    text_moves()
+    give_back(5)
+    text_pass_on()
+    near_sum()
+
+    held["core_own"].wait_recv()
+    for move in moves:
+        move[1]()
     text_out[...] = (
         text_sum[pl.ds(0, rows), :]
-        + text_in[pl.ds(0, rows), :]
+        + text_in[...]
         + text_back[pl.ds(0, rows), :].astype(jnp.float32)
         + text_back[pl.ds(rows, rows), :].astype(jnp.float32)
     )
@@ -251,13 +312,13 @@
         image_out[part, :] = near_own[part, :] + back_in[part, :].astype(jnp.float32)
     for copy in started:
         copy.wait_send()
-    for move in (up, down, text_up, text_down):
+    for move in (up, down, *moves):
         move[2]()
 
 
 def body(image_embeds, text_embeds, logit_scale, logit_bias):
     rows, width = image_embeds.shape
-    copies = len(CHUNKS) + 12 + 3 + 3 + 3 * len(CHUNKS) * 2 + len(CHUNKS) + 1 + 3 + 2
+    copies = len(CHUNKS) + 12 + 3 + 3 + 3 * len(CHUNKS) * 2 + len(CHUNKS) + 1 + 3 + 2 + 1
     half = lambda count: pltpu.VMEM((count * rows, width), jnp.bfloat16)
     full = lambda count: pltpu.VMEM((count * rows, width), jnp.float32)
     smem = pl.BlockSpec(memory_space=pltpu.SMEM)
@@ -269,8 +330,8 @@
         in_specs=[smem, smem, anywhere, anywhere],
         out_specs=[vmem, vmem],
         scratch_shapes=[
-            half(6), half(4), half(4), full(6), full(3), half(2), half(2),
-            half(2), full(1), half(3), half(3), full(1), half(3), half(3), half(1), half(1),
+            half(6), half(4), half(4), full(6), full(1), half(2), half(2), half(2), half(2),
+            half(3), full(1), half(3), half(3), full(1), half(3), half(3), half(1), half(1),
             pltpu.SemaphoreType.DMA((copies,)),
             pltpu.SemaphoreType.DMA((copies,)),
             pltpu.SemaphoreType.DMA((2,)),

time: 79.5 us -> 77.1 us (0.970)
  the two profiles are of different devices: /device:TPU:32 before, /device:TPU:24 now
where the time goes in v3:
time: 77.1 us; the launch traced here: 76.5 us
  Pallas kernels  71.7 us (93%)
  between operations  1.94 us (3%)
  local copies, waits for them, and re-layouts  1.86 us (2%)
  other arithmetic  0.97 us (1%)
    pallas_call x1, Pallas kernels, body(): pl.pallas_call(kernel, out_shape=[jax.ShapeDtypeStruct((rows, width), jnp...  71.7 us
    unnamed x4, local copies, waits for them, and re-layouts  1.86 us

profile of v3, /device:TPU:24, one launch (start us, length us, event | category | flops | bytes accessed | tf_op | source)
XLA Modules:
  0.0 76.5 jit_solution(8461965904861869463)
XLA Ops:
  1.9 0.0 copy-start
  1.9 0.9 %copy-done = bf16[96,1152]{1,0:T(8,128)(2,1)S(1)} copy-done((bf16[96,1152]{1,0:T(8,128)(2,1)S(1)}, bf16[96,1152]{1,0:T(8,128)(2,1)}, u32[]{:S(2)}) %copy-start) | copy-done | bytes 221208
  2.9 0.0 copy-start.1
  2.9 0.9 %copy-done.1 = bf16[96,1152]{1,0:T(8,128)(2,1)S(1)} copy-done((bf16[96,1152]{1,0:T(8,128)(2,1)S(1)}, bf16[96,1152]{1,0:T(8,128)(2,1)}, u32[]{:S(2)}) %copy-start.1) | copy-done | bytes 221208
  3.8 71.7 %shard_map.59 = (f32[96,1152]{1,0:T(8,128)S(1)}, f32[96,1152]{1,0:T(8,128)S(1)}) custom-call(f32[1]{0:T(128)} %copy.6.gain_ref, f32[1]{0:T(128)S(6)} %copy.7.bias_ref, bf16[96,1152]{1,0:T(8,128)(2,1)S(1)} %copy-done, bf16[96,1152]{1,0:T(8,128)(2,1)S(1)} %copy-done.1), custom_call_target="tpu_custom_call" | custom-call | flops 3057647616 | bytes 1769472 | tf_op jit(solution)/shard_map/pallas_call | solution.py:327
  75.6 1.0 %broadcast_multiply_fusion = (f32[96,1152]{1,0:T(8,128)}, f32[96,1152]{1,0:T(8,128)}) fusion(f32[96,1152]{1,0:T(8,128)S(1)} %get-tuple-element.5, f32[]{:T(128)} %bitcast.1, f32[96,1152]{1,0:T(8,128)S(1)} %get-tuple-element.4), kind=kLoop, calls=%fused_computation | loop fusion | flops 221184 | bytes 1769476 | tf_op jit(solution)/shard_map/mul | solution.py:347
Async XLA Ops:
  1.9 0.9 %copy-start = (bf16[96,1152]{1,0:T(8,128)(2,1)S(1)}, bf16[96,1152]{1,0:T(8,128)(2,1)}, u32[]{:S(2)}) copy-start(bf16[96,1152]{1,0:T(8,128)(2,1)} %image_ref.1) | copy-start | bytes 663556
  2.9 0.9 %copy-start.1 = (bf16[96,1152]{1,0:T(8,128)(2,1)S(1)}, bf16[96,1152]{1,0:T(8,128)(2,1)}, u32[]{:S(2)}) copy-start(bf16[96,1152]{1,0:T(8,128)(2,1)} %text_ref.1) | copy-start | bytes 663556

commit v4 on v3

--- a/solution.py
+++ b/solution.py
@@ -266,12 +266,12 @@
         near_own[...] = total
 
     pass_on()
-    text_from_below()
-    text_from_above()
     further_out(2)
     further_out(3)
     further_out(4)
     further_out(5)
+    text_from_below()
+    text_from_above()
     gather(0)
     gather(1)
     work_near()
@@ -292,8 +292,8 @@
     text_to_core()
     give_back(4)
     near_scatter()
+    give_back(5)
     text_moves()
-    give_back(5)
     text_pass_on()
     near_sum()
 

time: 77.1 us -> 75.3 us (0.977)
  Pallas kernels: 71.7 us -> 70.4 us
    pallas_call x1, Pallas kernels: 71.7 us -> 70.4 us  [body(): pl.pallas_call(kernel, out_shape=[jax.ShapeDtypeStruct((rows, width), jnp...]
where the time goes in v4:
time: 75.3 us; the launch traced here: 75.2 us
  Pallas kernels  70.4 us (93%)
  between operations  1.94 us (3%)
  local copies, waits for them, and re-layouts  1.86 us (2%)
  other arithmetic  0.97 us (1%)
    pallas_call x1, Pallas kernels, body(): pl.pallas_call(kernel, out_shape=[jax.ShapeDtypeStruct((rows, width), jnp...  70.4 us
    unnamed x4, local copies, waits for them, and re-layouts  1.86 us

profile of v4, /device:TPU:24, one launch (start us, length us, event | category | flops | bytes accessed | tf_op | source)
XLA Modules:
  0.0 75.2 jit_solution(9925016110405425448)
XLA Ops:
  1.9 0.0 copy-start
  1.9 0.9 %copy-done = bf16[96,1152]{1,0:T(8,128)(2,1)S(1)} copy-done((bf16[96,1152]{1,0:T(8,128)(2,1)S(1)}, bf16[96,1152]{1,0:T(8,128)(2,1)}, u32[]{:S(2)}) %copy-start) | copy-done | bytes 221208
  2.9 0.0 copy-start.1
  2.9 0.9 %copy-done.1 = bf16[96,1152]{1,0:T(8,128)(2,1)S(1)} copy-done((bf16[96,1152]{1,0:T(8,128)(2,1)S(1)}, bf16[96,1152]{1,0:T(8,128)(2,1)}, u32[]{:S(2)}) %copy-start.1) | copy-done | bytes 221208
  3.8 70.4 %shard_map.59 = (f32[96,1152]{1,0:T(8,128)S(1)}, f32[96,1152]{1,0:T(8,128)S(1)}) custom-call(f32[1]{0:T(128)} %copy.6.gain_ref, f32[1]{0:T(128)S(6)} %copy.7.bias_ref, bf16[96,1152]{1,0:T(8,128)(2,1)S(1)} %copy-done, bf16[96,1152]{1,0:T(8,128)(2,1)S(1)} %copy-done.1), custom_call_target="tpu_custom_call" | custom-call | flops 3057647616 | bytes 1769472 | tf_op jit(solution)/shard_map/pallas_call | solution.py:327
  74.2 1.0 %broadcast_multiply_fusion = (f32[96,1152]{1,0:T(8,128)}, f32[96,1152]{1,0:T(8,128)}) fusion(f32[96,1152]{1,0:T(8,128)S(1)} %get-tuple-element.5, f32[]{:T(128)} %bitcast.1, f32[96,1152]{1,0:T(8,128)S(1)} %get-tuple-element.4), kind=kLoop, calls=%fused_computation | loop fusion | flops 221184 | bytes 1769476 | tf_op jit(solution)/shard_map/mul | solution.py:347
Async XLA Ops:
  1.9 0.9 %copy-start = (bf16[96,1152]{1,0:T(8,128)(2,1)S(1)}, bf16[96,1152]{1,0:T(8,128)(2,1)}, u32[]{:S(2)}) copy-start(bf16[96,1152]{1,0:T(8,128)(2,1)} %image_ref.1) | copy-start | bytes 663556
  2.9 0.9 %copy-start.1 = (bf16[96,1152]{1,0:T(8,128)(2,1)S(1)}, bf16[96,1152]{1,0:T(8,128)(2,1)}, u32[]{:S(2)}) copy-start(bf16[96,1152]{1,0:T(8,128)(2,1)} %text_ref.1) | copy-start | bytes 663556

commit v5 on v4

--- a/solution.py
+++ b/solution.py
@@ -291,8 +291,8 @@
     work(5)
     text_to_core()
     give_back(4)
+    give_back(5)
     near_scatter()
-    give_back(5)
     text_moves()
     text_pass_on()
     near_sum()

time: 75.3 us -> 75.3 us (level)
  no operation moved by 1% of the time
where the time goes in v5:
time: 75.3 us; the launch traced here: 75.1 us
  Pallas kernels  70.4 us (93%)
  between operations  1.94 us (3%)
  local copies, waits for them, and re-layouts  1.86 us (2%)
  other arithmetic  0.97 us (1%)
    pallas_call x1, Pallas kernels, body(): pl.pallas_call(kernel, out_shape=[jax.ShapeDtypeStruct((rows, width), jnp...  70.4 us
    unnamed x4, local copies, waits for them, and re-layouts  1.86 us

profile of v5, /device:TPU:24, one launch (start us, length us, event | category | flops | bytes accessed | tf_op | source)
XLA Modules:
  0.0 75.1 jit_solution(13850575980541477830)
XLA Ops:
  1.9 0.0 copy-start
  1.9 0.9 %copy-done = bf16[96,1152]{1,0:T(8,128)(2,1)S(1)} copy-done((bf16[96,1152]{1,0:T(8,128)(2,1)S(1)}, bf16[96,1152]{1,0:T(8,128)(2,1)}, u32[]{:S(2)}) %copy-start) | copy-done | bytes 221208
  2.9 0.0 copy-start.1
  2.9 0.9 %copy-done.1 = bf16[96,1152]{1,0:T(8,128)(2,1)S(1)} copy-done((bf16[96,1152]{1,0:T(8,128)(2,1)S(1)}, bf16[96,1152]{1,0:T(8,128)(2,1)}, u32[]{:S(2)}) %copy-start.1) | copy-done | bytes 221208
  3.8 70.4 %shard_map.59 = (f32[96,1152]{1,0:T(8,128)S(1)}, f32[96,1152]{1,0:T(8,128)S(1)}) custom-call(f32[1]{0:T(128)} %copy.6.gain_ref, f32[1]{0:T(128)S(6)} %copy.7.bias_ref, bf16[96,1152]{1,0:T(8,128)(2,1)S(1)} %copy-done, bf16[96,1152]{1,0:T(8,128)(2,1)S(1)} %copy-done.1), custom_call_target="tpu_custom_call" | custom-call | flops 3057647616 | bytes 1769472 | tf_op jit(solution)/shard_map/pallas_call | solution.py:327
  74.2 1.0 %broadcast_multiply_fusion = (f32[96,1152]{1,0:T(8,128)}, f32[96,1152]{1,0:T(8,128)}) fusion(f32[96,1152]{1,0:T(8,128)S(1)} %get-tuple-element.5, f32[]{:T(128)} %bitcast.1, f32[96,1152]{1,0:T(8,128)S(1)} %get-tuple-element.4), kind=kLoop, calls=%fused_computation | loop fusion | flops 221184 | bytes 1769476 | tf_op jit(solution)/shard_map/mul | solution.py:347
Async XLA Ops:
  1.9 0.9 %copy-start = (bf16[96,1152]{1,0:T(8,128)(2,1)S(1)}, bf16[96,1152]{1,0:T(8,128)(2,1)}, u32[]{:S(2)}) copy-start(bf16[96,1152]{1,0:T(8,128)(2,1)} %image_ref.1) | copy-start | bytes 663556
  2.9 0.9 %copy-start.1 = (bf16[96,1152]{1,0:T(8,128)(2,1)S(1)}, bf16[96,1152]{1,0:T(8,128)(2,1)}, u32[]{:S(2)}) copy-start(bf16[96,1152]{1,0:T(8,128)(2,1)} %text_ref.1) | copy-start | bytes 663556
